TPU v7x, 32 devices: a whole 2x2x4 slice. The times are simulated.
32 devices in a mesh: space: 16 (over z, y, core), mem: 2 (over x).
Axes of the slice: x: 2, y: 2, z: 4, core: 2. Of those that a mesh axis runs over, the one named last changes fastest.
Arguments:
- state: float32 [64, 262144], P('mem', 'space'), may hold values from -6 to 6
- obs_index: int32 [4, 4096], P(None, 'space'), may hold values from 0 to 262143, as said below
- obs_value: float32 [4, 4096], P(None, 'space'), may hold values from -8 to 8
- obs_var: float32 [4, 4096], P(None, 'space'), may hold values from 0.02 to 5
Outputs:
- posterior: float32 [64, 262144], P('mem', 'space')
Inputs may be any that keep to these rules, and one draw needn't show every extreme that they name: `obs_index`: observation k of every batch measures a column of the block owned by index k // 256 of space, that is a column between (k // 256) * 16384 and (k // 256 + 1) * 16384 - 1.
All inputs are finite; a program needn't handle non-finite values.
Results may differ from a plain program's by a relative error of at most 0.0075.
Values may be sent and summed in bfloat16 or wider, within the bound.
A program may use at most 64 MiB of HBM per device.

v0:
```python
import functools

import jax
import jax.numpy as jnp
from jax import lax
from jax.experimental import pallas as pl
from jax.experimental.pallas import tpu as pltpu
from jax.sharding import PartitionSpec as P

RADIUS = 32768
OFFSETS = (-2, 2, -1, 1)
SLOT = {-2: 0, 0: 1, 2: 2, -1: 3, 1: 4}
CHUNK = 256
SPAN = 512
SIDES = ((1, True), (1, False), (0, False), (2, True))
GROUP = 64
PARTS = 2
f32, bf16 = jnp.float32, jnp.bfloat16


def gather_kernel(idx_ref, state_ref, pos_ref, value_ref, var_ref, out_ref, row_ref):
    half_members, cols = state_ref.shape
    batches, obs_dev = idx_ref.shape
    base = lax.axis_index("space") * cols
    lanes = lax.broadcasted_iota(jnp.int32, (half_members, 128), 1)
    along = lax.broadcasted_iota(jnp.int32, (obs_dev, obs_dev), 1)
    down = lax.broadcasted_iota(jnp.int32, (obs_dev, obs_dev), 0)
    for batch in range(batches):
        parts = []
        for part in range(obs_dev // 128):
            def pick(step, acc):
                for inner in range(32):
                    t = step * 32 + inner
                    col = idx_ref[batch, part * 128 + t] - base
                    hi = lax.shift_right_logical(col, 7)
                    lo = col & 127
                    tile = state_ref[:, pl.ds(pl.multiple_of(hi * 128, 128), 128)]
                    moved = pltpu.roll(tile, (t - lo) & 127, 1)
                    acc = jnp.where(lanes == t, moved, acc)
                return acc
            parts.append(lax.fori_loop(0, 4, pick, jnp.zeros((half_members, 128), f32)))
        q = (pos_ref[batch:batch + 1, :] - base - cols // 2).astype(f32) * (1.0 / RADIUS)
        each = jnp.broadcast_to(q, (obs_dev, obs_dev))
        mine = jnp.transpose(each)
        before = (each < mine) | ((each == mine) & (along < down))
        rank = jnp.sum(jnp.where(before, 1.0, 0.0), axis=1, keepdims=True)
        order = jnp.where(rank == along.astype(f32), 1.0, 0.0)
        rows = jnp.concatenate(
            [jnp.concatenate(parts, axis=1), q, value_ref[batch:batch + 1, :],
             var_ref[batch:batch + 1, :], jnp.zeros((5, obs_dev), f32)], axis=0)
        placed = jnp.dot(
            rows, order, precision=lax.Precision.HIGHEST, preferred_element_type=f32)
        out_ref[:, batch * obs_dev:(batch + 1) * obs_dev] = placed[:half_members]
        row_ref[batch] = placed[half_members:]


def kernel(
    n_space, batches, obs_dev, half_members, cols,
    g_send, state_ref, row_ref, got_ref, awt_out, moment_out, c_out,
    g_recv, g_ref, x_send, x_recv,
    pos_own, pos_nb, aw, coef,
    g_sems, x_sems, pos_ssem, pos_rsem, aw_ssem, aw_rsem,
):
    space = lax.axis_index("space")
    mem = lax.axis_index("mem")
    other = 1 - mem
    width = cols // 2
    members = 2 * half_members
    own_start = mem * width
    other_start = other * width
    base = space * cols
    block = cols / RADIUS
    partner = {"mem": other}
    valid = {o: (space + o >= 0) & (space + o < n_space) for o in OFFSETS}

    barrier = pltpu.get_barrier_semaphore()
    pl.semaphore_signal(barrier, inc=1, device_id=partner, device_id_type=pl.DeviceIdType.MESH)
    for o in OFFSETS:
        @pl.when(valid[o])
        def _(o=o):
            pl.semaphore_signal(
                barrier, inc=1, device_id={"space": space + o},
                device_id_type=pl.DeviceIdType.MESH)

    def g_copy(part):
        span = pl.ds(0, obs_dev) if part == 0 else pl.ds(obs_dev, (batches - 1) * obs_dev)
        return pltpu.make_async_remote_copy(
            src_ref=g_send.at[:, span], dst_ref=g_recv.at[:, span],
            send_sem=g_sems.at[0, part], recv_sem=g_sems.at[1, part],
            device_id=partner, device_id_type=pl.DeviceIdType.MESH)

    x_copy = pltpu.make_async_remote_copy(
        src_ref=x_send, dst_ref=x_recv, send_sem=x_sems.at[0], recv_sem=x_sems.at[1],
        device_id=partner, device_id_type=pl.DeviceIdType.MESH)

    def pos_copy(o):
        i = OFFSETS.index(o)
        back = OFFSETS.index(-o)
        return pltpu.make_async_remote_copy(
            src_ref=pos_own, dst_ref=pos_nb.at[back],
            send_sem=pos_ssem.at[i], recv_sem=pos_rsem.at[back],
            device_id={"space": space + o}, device_id_type=pl.DeviceIdType.MESH)

    def pos_wait(o):
        i = OFFSETS.index(o)
        pltpu.make_async_remote_copy(
            src_ref=pos_own, dst_ref=pos_nb.at[i],
            send_sem=pos_ssem.at[i], recv_sem=pos_rsem.at[i],
            device_id={"space": space + o}, device_id_type=pl.DeviceIdType.MESH).wait_recv()

    def aw_copy(batch, o):
        i = OFFSETS.index(o)
        back = OFFSETS.index(-o)
        return pltpu.make_async_remote_copy(
            src_ref=aw.at[batch, SLOT[0]], dst_ref=aw.at[batch, SLOT[-o]],
            send_sem=aw_ssem.at[batch, i], recv_sem=aw_rsem.at[batch, back],
            device_id={"space": space + o}, device_id_type=pl.DeviceIdType.MESH)

    def aw_wait(batch, o):
        i = OFFSETS.index(o)
        pltpu.make_async_remote_copy(
            src_ref=aw.at[batch, SLOT[0]], dst_ref=aw.at[batch, SLOT[o]],
            send_sem=aw_ssem.at[batch, i], recv_sem=aw_rsem.at[batch, i],
            device_id={"space": space + o}, device_id_type=pl.DeviceIdType.MESH).wait_recv()

    pos_own[...] = jnp.zeros_like(pos_own)
    for batch in range(batches):
        pos_own[batch:batch + 1, :] = row_ref[batch, 0:1, :]
    for o in OFFSETS:
        @pl.when(jnp.logical_not(valid[o]))
        def _(o=o):
            pos_nb[OFFSETS.index(o)] = jnp.zeros(pos_nb.shape[1:], f32)
            for batch in range(batches):
                aw[batch, SLOT[o]] = jnp.zeros(aw.shape[2:], bf16)

    count = 1
    for o in OFFSETS:
        count = count + jnp.where(valid[o], 1, 0)
    pl.semaphore_wait(barrier, count)
    g_copy(0).start()
    for o in OFFSETS:
        @pl.when(valid[o])
        def _(o=o):
            pos_copy(o).start()

    def cast(i, carry):
        at = pl.multiple_of(i * 1024, 128)
        x_send[:, pl.ds(at, 1024)] = state_ref[
            :, pl.ds(pl.multiple_of(other_start + at, 128), 1024)].astype(bf16)
        return carry
    lax.fori_loop(0, width // 1024, cast, 0)
    x_copy.start()
    g_copy(1).start()
    g_ref[:half_members, :] = g_send[...]

    def increment(batch, now, u):
        mean = jnp.sum(now, axis=0, keepdims=True) * (1.0 / members)
        anomaly = now - mean
        spread = anomaly.astype(bf16)
        total = jnp.dot(
            moment_out[batch].astype(bf16),
            jnp.concatenate(
                [spread, (anomaly * u).astype(bf16), (anomaly * (u * u)).astype(bf16)], axis=0),
            preferred_element_type=f32)
        for slot in range(3):
            cov = jnp.dot(
                awt_out[batch, slot * obs_dev:(slot + 1) * obs_dev, :members], spread, preferred_element_type=f32)
            c = coef[slot]
            if slot == 0:
                t = jnp.maximum(c - u, 0.0)
            elif slot == 1:
                t = jnp.maximum(1.0 - jnp.abs(c - u), 0.0)
            else:
                t = jnp.maximum(c + u, 0.0)
            gain = (t * t * cov).astype(bf16)
            total = total + jnp.dot(
                aw[batch, slot, members:2 * members, :], gain, preferred_element_type=f32)
        return total

    def build(batch):
        def row(o):
            if o == 0:
                return pos_own[batch:batch + 1, :]
            return pos_nb[OFFSETS.index(o), batch:batch + 1, :] + o * block
        for o in (-2, 0, 2):
            slot = SLOT[o]
            q = row(o)
            c = q if o == 0 else (1.0 + q if o < 0 else 1.0 - q)
            coef[slot] = jnp.transpose(jnp.broadcast_to(c, (CHUNK, obs_dev)))
            c_out[batch, slot:slot + 1, :] = c
            awt_out[batch, slot * obs_dev:(slot + 1) * obs_dev, :] = jnp.transpose(
                aw[batch, slot].astype(f32)).astype(bf16)
        sums = 0.0
        for o in (-1, 1):
            slot = SLOT[o]
            q = row(o)
            c = 1.0 + q if o < 0 else 1.0 - q
            a = aw[batch, slot, :members, :].astype(f32)
            rhs = jnp.concatenate([a * (c * c), a * (2.0 * o * c), a], axis=0).astype(bf16)
            sums = sums + lax.dot_general(
                aw[batch, slot, members:2 * members, :], rhs, (((1,), (1,)), ((), ())),
                preferred_element_type=f32)
        moment_out[batch] = sums

    def summarize(batch):
        span = slice(batch * obs_dev, (batch + 1) * obs_dev)
        prior = g_ref[:, span]
        values = row_ref[batch, 1:2, :]
        variances = row_ref[batch, 2:3, :]
        obs_mean = jnp.sum(prior, axis=0, keepdims=True) * (1.0 / members)
        anomaly = prior - obs_mean
        spread = jnp.sum(anomaly * anomaly, axis=0, keepdims=True) * (1.0 / (members - 1)) + 1e-06
        post_var = 1.0 / (1.0 / spread + 1.0 / variances)
        post_mean = post_var * (obs_mean / spread + values / variances)
        change = post_mean - obs_mean + (jnp.sqrt(post_var / spread) - 1.0) * anomaly
        aw[batch, SLOT[0], :members, :] = anomaly.astype(bf16)
        aw[batch, SLOT[0], members:, :] = (change / ((members - 1) * spread)).astype(bf16)

    for batch in range(batches):
        if batch == 0:
            g_copy(0).wait_recv()
            g_ref[half_members:, :obs_dev] = g_recv[:, :obs_dev]
        summarize(batch)
        for o in OFFSETS:
            @pl.when(valid[o])
            def _(o=o):
                aw_copy(batch, o).start()
        if batch == 0:
            g_copy(1).wait_recv()
            g_ref[half_members:, obs_dev:] = g_recv[:, obs_dev:]
            for o in OFFSETS:
                @pl.when(valid[o])
                def _(o=o):
                    pos_wait(o)
        for o in OFFSETS:
            @pl.when(valid[o])
            def _(o=o):
                aw_wait(batch, o)
        build(batch)
        for later in range(batch + 1, batches):
            span = slice(later * obs_dev, (later + 1) * obs_dev)
            now = g_ref[:, span]
            g_ref[:, span] = now + increment(batch, now, pos_own[later:later + 1, :])
    x_copy.wait_recv()
    got_ref[...] = x_recv[...]

    g_copy(0).wait_send()
    g_copy(1).wait_send()
    x_copy.wait_send()
    for o in OFFSETS:
        @pl.when(valid[o])
        def _(o=o):
            pos_copy(o).wait_send()
            for batch in range(batches):
                aw_copy(batch, o).wait_send()


def update_kernel(
    first, bound_ref, state_ref, got_ref, awt_ref, moment_ref, c_ref,
    own_ref, sent_ref, cur, coef, table,
):
    half_members, cols = state_ref.shape
    batches, obs_dev = c_ref.shape[0], c_ref.shape[2]
    members = 2 * half_members
    part_width = own_ref.shape[1]
    start = lax.axis_index("mem") * (cols // 2) + first
    chunks = part_width // SPAN
    lane_u = lax.broadcasted_iota(jnp.int32, (1, SPAN), 1)
    count = cols // 2 // SPAN
    groups = obs_dev // GROUP

    def span_of(i):
        return pl.ds(pl.multiple_of(i * SPAN, SPAN), SPAN)

    def load(i, carry):
        cur[:half_members, span_of(i)] = state_ref[
            :, pl.ds(pl.multiple_of(start + i * SPAN, SPAN), SPAN)]
        cur[half_members:, span_of(i)] = got_ref[:, span_of(first // SPAN + i)].astype(f32)
        return carry
    lax.fori_loop(0, chunks, load, 0)

    def assimilate(batch, carry):
        for slot in range(3):
            coef[slot] = jnp.transpose(
                jnp.broadcast_to(c_ref[batch, slot:slot + 1, :], (128, obs_dev)))

        for side, (slot, left) in enumerate(SIDES):
            total = moment_ref[batch] if side == 0 else jnp.zeros((members, 3 * members), f32)
            for step in range(groups):
                g = step if left else groups - 1 - step
                table[side, g if left else g + 1] = total
                rows = slice(g * GROUP, (g + 1) * GROUP)
                pair = awt_ref[batch, pl.ds(slot * obs_dev + g * GROUP, GROUP), :]
                a = pair[:, :members].astype(f32)
                c = coef[slot, rows, :members]
                if slot == 1:
                    c = 1.0 + c if left else 1.0 - c
                sign = -2.0 if (slot == 0 or (slot == 1 and left)) else 2.0
                rhs = jnp.concatenate([a * (c * c), a * (sign * c), a], axis=1).astype(bf16)
                total = total + lax.dot_general(
                    pair[:, members:], rhs, (((0,), (0,)), ((), ())),
                    preferred_element_type=f32)
            table[side, groups if left else 0] = total

        def taper_of(slot, c, u):
            c = jnp.concatenate([c] * (SPAN // 128), axis=1)
            if slot == 0:
                t = jnp.maximum(c - u, 0.0)
            elif slot == 1:
                t = jnp.maximum(1.0 - jnp.abs(c - u), 0.0)
            else:
                t = jnp.maximum(c + u, 0.0)
            return t * t

        def chunk(i):
            now = cur[:, span_of(i)]
            mean = jnp.sum(now, axis=0, keepdims=True) * (1.0 / members)
            anomaly = now - mean
            spread = anomaly.astype(bf16)
            u = (lane_u + (start + i * SPAN - cols // 2)).astype(f32) * (1.0 / RADIUS)
            pairs, tapers, bounds = [], [], []
            for slot in range(3):
                at = (slot * 2) * count + first // SPAN + i
                low = jnp.minimum(bound_ref[batch, at] // GROUP, groups - 1)
                high = jnp.maximum(
                    (bound_ref[batch, at + count] + GROUP - 1) // GROUP, low + 1)
                bounds.append((low, high))
                pairs.append(awt_ref[
                    batch, pl.ds(pl.multiple_of(slot * obs_dev + low * GROUP, GROUP), GROUP), :])
                tapers.append(taper_of(
                    slot, coef[slot, pl.ds(pl.multiple_of(low * GROUP, GROUP), GROUP), :], u))
            mix = sum(table[side, bounds[slot][0 if left else 1]]
                      for side, (slot, left) in enumerate(SIDES))
            pair = jnp.concatenate(pairs, axis=0)
            cov = jnp.dot(pair[:, :members], spread, preferred_element_type=f32)
            gain = (jnp.concatenate(tapers, axis=0) * cov).astype(bf16)
            total = now + jnp.dot(
                mix.astype(bf16),
                jnp.concatenate(
                    [spread, (anomaly * u).astype(bf16), (anomaly * (u * u)).astype(bf16)],
                    axis=0),
                preferred_element_type=f32)
            total = total + lax.dot_general(
                pair[:, members:], gain, (((0,), (0,)), ((), ())), preferred_element_type=f32)
            return total, spread, u, bounds

        def more_groups(i, spread, u, bounds):
            for slot in range(3):
                def dense(g, more):
                    rows = pl.ds(pl.multiple_of(slot * obs_dev + g * GROUP, GROUP), GROUP)
                    pair = awt_ref[batch, rows, :]
                    cov = jnp.dot(pair[:, :members], spread, preferred_element_type=f32)
                    c = coef[slot, pl.ds(pl.multiple_of(g * GROUP, GROUP), GROUP), :]
                    gain = (taper_of(slot, c, u) * cov).astype(bf16)
                    cur[:, span_of(i)] += lax.dot_general(
                        pair[:, members:], gain, (((0,), (0,)), ((), ())),
                        preferred_element_type=f32)
                    return more
                lax.fori_loop(bounds[slot][0] + 1, bounds[slot][1], dense, 0)

        def two(step, inner):
            both = [chunk(2 * step + k) for k in range(2)]
            for k in range(2):
                cur[:, span_of(2 * step + k)] = both[k][0]
            for k in range(2):
                more_groups(2 * step + k, *both[k][1:])
            return inner
        lax.fori_loop(0, chunks // 2, two, 0)
        return carry
    lax.fori_loop(0, batches, assimilate, 0)

    def store(i, carry):
        own_ref[:, span_of(i)] = cur[:half_members, span_of(i)]
        sent_ref[:, span_of(i)] = (
            cur[half_members:, span_of(i)]
            - got_ref[:, span_of(first // SPAN + i)].astype(f32)).astype(bf16)
        return carry
    lax.fori_loop(0, chunks, store, 0)


def shards(n_space, state, obs_index, obs_value, obs_var):
    half_members, cols = state.shape
    batches, obs_dev = obs_index.shape
    members, width = 2 * half_members, cols // 2
    vmem = pl.BlockSpec(memory_space=pltpu.VMEM)
    smem = pl.BlockSpec(memory_space=pltpu.SMEM)
    n_obs = batches * obs_dev
    dma = pltpu.SemaphoreType.DMA
    shape = jax.ShapeDtypeStruct
    gathered, rows = pl.pallas_call(
        gather_kernel,
        out_shape=(shape((half_members, n_obs), f32), shape((batches, 8, obs_dev), f32)),
        in_specs=[smem, vmem, vmem, vmem, vmem],
        out_specs=(vmem, vmem),
        compiler_params=pltpu.CompilerParams(vmem_limit_bytes=32 * 1024 * 1024),
    )(obs_index, state, obs_index, obs_value, obs_var)
    got, awt, moments, c_rows = pl.pallas_call(
        functools.partial(kernel, n_space, batches, obs_dev, half_members, cols),
        out_shape=(
            shape((half_members, width), bf16),
            shape((batches, 3 * obs_dev, 2 * members), bf16),
            shape((batches, members, 3 * members), f32),
            shape((batches, 8, obs_dev), f32),
        ),
        in_specs=[vmem] * 3,
        out_specs=(vmem,) * 4,
        scratch_shapes=[
            pltpu.VMEM((half_members, n_obs), f32),
            pltpu.VMEM((members, n_obs), f32),
            pltpu.VMEM((half_members, width), bf16),
            pltpu.VMEM((half_members, width), bf16),
            pltpu.VMEM((8, obs_dev), f32),
            pltpu.VMEM((4, 8, obs_dev), f32),
            pltpu.VMEM((batches, 5, 2 * members, obs_dev), bf16),
            pltpu.VMEM((3, obs_dev, CHUNK), f32),
            dma((2, 2)), dma((2,)), dma((4,)), dma((4,)),
            dma((batches, 4)), dma((batches, 4)),
        ],
        compiler_params=pltpu.CompilerParams(
            collective_id=0, has_side_effects=True, vmem_limit_bytes=32 * 1024 * 1024),
    )(gathered, state, rows)
    mem = lax.axis_index("mem")
    turn = c_rows[:, :3, :] * jnp.array([1.0, 1.0, -1.0], f32)[None, :, None]
    edges = (mem * width - width + SPAN * lax.iota(jnp.int32, width // SPAN)).astype(f32) / RADIUS
    edges = edges[None, None, :, None]
    low = jnp.sum((turn[:, :, None, :] <= edges).astype(jnp.int32), axis=3)
    high = jnp.sum((turn[:, :, None, :] < edges + (SPAN - 1) / RADIUS).astype(jnp.int32), axis=3)
    bounds = jnp.stack([low, jnp.maximum(low, high)], axis=2).reshape(batches, -1)
    part_width = width // PARTS
    own, come = [], []
    for part in range(PARTS):
        kept, sent = pl.pallas_call(
            functools.partial(update_kernel, part * part_width),
            out_shape=(
                shape((half_members, part_width), f32), shape((half_members, part_width), bf16)),
            in_specs=[smem] + [vmem] * 5,
            out_specs=(vmem, vmem),
            scratch_shapes=[
                pltpu.VMEM((members, part_width), f32), pltpu.VMEM((3, obs_dev, 128), f32),
                pltpu.VMEM((4, obs_dev // GROUP + 1, members, 3 * members), f32)],
            compiler_params=pltpu.CompilerParams(vmem_limit_bytes=32 * 1024 * 1024),
            cost_estimate=pl.CostEstimate(
                flops=12 * 10**9 // PARTS, bytes_accessed=4 * 2**20, transcendentals=0),
        )(bounds, state, got, awt, moments, c_rows)
        own.append(kept)
        come.append(lax.ppermute(sent, "mem", [(0, 1), (1, 0)]))
    own = jnp.concatenate(own, axis=1)
    come = jnp.concatenate(come, axis=1).astype(f32)
    return jnp.where(
        mem == 0,
        jnp.concatenate([own, state[:, width:] + come], axis=1),
        jnp.concatenate([state[:, :width] + come, own], axis=1))


def solution(mesh):
    placed = (P("mem", "space"), P(None, "space"), P(None, "space"), P(None, "space"))
    return jax.shard_map(
        functools.partial(shards, mesh.shape["space"]), mesh=mesh, in_specs=placed,
        out_specs=P("mem", "space"), check_vma=False)
```

profile of v0, /device:TPU:16, one launch (start us, length us, event | category | flops | bytes accessed | tf_op | source)
XLA Modules:
  0.0 100.8 jit_solution(13254703363195898830)
XLA Ops:
  0.0 0.0 copy-start
  0.0 1.6 %copy-done = f32[32,16384]{1,0:T(8,128)S(1)} copy-done((f32[32,16384]{1,0:T(8,128)S(1)}, f32[32,16384]{1,0:T(8,128)}, u32[]{:S(2)}) %copy-start) | copy-done | bytes 2097176
  1.6 0.0 copy-start.2
  1.6 0.7 copy-done.2
  2.3 0.0 copy-start.3
  2.3 0.7 copy-done.3
  3.0 0.0 copy-start.4
  3.0 0.7 copy-done.4
  3.7 0.0 copy-start.1
  3.7 0.0 copy-start.9
  3.7 9.3 %shard_map.55 = (f32[32,1024]{1,0:T(8,128)S(1)}, f32[4,8,256]{2,1,0:T(8,128)S(1)}) custom-call(s32[4,256]{1,0:T(4,128)S(1)} %copy-done.2, f32[32,16384]{1,0:T(8,128)S(1)} %copy-done, s32[4,256]{1,0:T(4,128)S(1)} %copy-done.2, f32[4,256]{1,0:T(4,128)S(1)} %copy-done.3, f32[4,256]{1,0:T(4,128)S(1)} %copy-done.4), custom_call_target="tpu_custom_call" | custom-call | tf_op jit(solution)/shard_map/pallas_call | solution.py:390
  13.0 0.0 copy-done.1
  13.0 38.5 %shard_map.56 = (bf16[32,8192]{1,0:T(8,128)(2,1)S(1)}, bf16[4,768,128]{2,1,0:T(8,128)(2,1)S(1)}, f32[4,64,192]{2,1,0:T(8,128)S(1)}, f32[4,8,256]{2,1,0:T(8,128)S(1)}) custom-call(f32[32,1024]{1,0:T(8,128)S(1)} %get-tuple-element.15.g_send, f32[32,16384]{1,0:T(8,128)S(1)} %copy-done.1, f32[4,8,256]{2,1,0:T(8,128)S(1)} %get-tuple-element.16.row_ref), custom_call_target="tpu_custom_call" | custom-call | tf_op jit(solution)/shard_map/pallas_call | solution.py:397
  51.5 0.0 copy-start.5
  51.5 0.9 copy-done.5
  52.3 0.0 copy-start.7
  52.4 0.0 copy-done.9
  52.4 0.1 slice_multiply_fusion
  52.4 0.6 convert_reduce_fusion
  53.0 0.1 reshape.27.bound_ref
  53.1 0.0 copy-start.6
  53.1 1.1 %copy-done.6 = bf16[4,768,128]{2,1,0:T(8,128)(2,1)S(1)} copy-done((bf16[4,768,128]{2,1,0:T(8,128)(2,1)S(1)}, bf16[4,768,128]{2,1,0:T(8,128)(2,1)}, u32[]{:S(2)}) %copy-start.6) | copy-done | bytes 786456
  54.3 15.7 %shard_map.58 = (f32[32,4096]{1,0:T(8,128)S(1)}, bf16[32,4096]{1,0:T(8,128)(2,1)}) custom-call(s32[4,96]{1,0:T(4,128)S(1)} %reshape.27.bound_ref, f32[32,16384]{1,0:T(8,128)S(1)} %copy-done.1, bf16[32,8192]{1,0:T(8,128)(2,1)S(1)} %get-tuple-element.18.got_ref, bf16[4,768,128]{2,1,0:T(8,128)(2,1)S(1)} %copy-done.6, ...), custom_call_target="tpu_custom_call" | custom-call | flops 6000000000 | bytes 4194304 | tf_op jit(solution)/shard_map/pallas_call | solution.py:432
  69.9 0.0 copy-done.7
  69.9 1.6 %collective-permute-start.1 = (bf16[32,4096]{1,0:T(8,128)(2,1)}, bf16[32,4096]{1,0:T(8,128)(2,1)}, u32[]{:S(2)}, u32[]{:S(2)}) collective-permute-start(bf16[32,4096]{1,0:T(8,128)(2,1)} %get-tuple-element.24), channel_id=1, source_target_pairs={{0,1},{1,0},{2,3},{3,2},{4,5},{5,4},{6,7},{7,6},{8,9},{9,8},{10,11... | collective-permute-start | bytes 786440 | tf_op jit(solution)/shard_map/ppermute | solution.py:446
  71.6 0.0 copy-start.8
  71.6 1.0 %copy-done.8 = bf16[32,8192]{1,0:T(8,128)(2,1)S(1)} copy-done((bf16[32,8192]{1,0:T(8,128)(2,1)S(1)}, bf16[32,8192]{1,0:T(8,128)(2,1)}, u32[]{:S(2)}) %copy-start.8) | copy-done | bytes 524312
  72.6 17.6 %shard_map.57 = (f32[32,4096]{1,0:T(8,128)S(1)}, bf16[32,4096]{1,0:T(8,128)(2,1)}) custom-call(s32[4,96]{1,0:T(4,128)S(1)} %reshape.27.bound_ref, f32[32,16384]{1,0:T(8,128)S(1)} %copy-done.1, bf16[32,8192]{1,0:T(8,128)(2,1)S(1)} %copy-done.8, bf16[4,768,128]{2,1,0:T(8,128)(2,1)S(1)} %copy-done.6, f32[4,64,192]{2,1,0:T(8,128)S(1)} %get-tuple-element.20.moment_ref, ...), custom_call_target="tpu_custom_call" | custom-call | flops 6000000000 | bytes 4194304 | tf_op jit(solution)/shard_map/pallas_call | solution.py:432
  90.2 0.0 collective-permute-start
  90.2 0.0 collective-permute-done.1
  90.2 7.8 %collective-permute-done = bf16[32,4096]{1,0:T(8,128)(2,1)S(1)} collective-permute-done((bf16[32,4096]{1,0:T(8,128)(2,1)}, bf16[32,4096]{1,0:T(8,128)(2,1)S(1)}, u32[]{:S(2)}, u32[]{:S(2)}) %collective-permute-start) | collective-permute-done | bytes 262176 | tf_op jit(solution)/shard_map/ppermute | solution.py:446
  98.1 1.1 %convert_add_fusion = (f32[32,8192]{1,0:T(8,128)S(1)}, f32[32,8192]{1,0:T(8,128)S(1)}) fusion(f32[32,16384]{1,0:T(8,128)S(1)} %copy-done.1, bf16[32,4096]{1,0:T(8,128)(2,1)} %collective-permute-done.1, bf16[32,4096]{1,0:T(8,128)(2,1)S(1)} %collective-permute-done), kind=kLoop, calls=%fused_computation.1 | loop fusion | flops 1572864 | bytes 4718592 | tf_op jit(solution)/shard_map/add | solution.py:452
  99.2 1.6 %maximum_select_fusion = f32[32,16384]{1,0:T(8,128)} fusion(f32[32,8192]{1,0:T(8,128)S(1)} %get-tuple-element.30, f32[32,4096]{1,0:T(8,128)S(1)} %get-tuple-element.22, f32[32,4096]{1,0:T(8,128)S(1)} %get-tuple-element.21, f32[32,8192]{1,0:T(8,128)S(1)} %get-tuple-element.29, pred[]{:T(512)S(6)} %eq.3), kind=kLoop, calls=%fused_computation | loop fusion | flops 2621440 | bytes 5242881 | tf_op jit(solution)/shard_map/jit(_where)/select_n | solution.py:449
  (4 shorter events, 0.0 us)
Async XLA Ops:
  0.0 1.6 %copy-start = (f32[32,16384]{1,0:T(8,128)S(1)}, f32[32,16384]{1,0:T(8,128)}, u32[]{:S(2)}) copy-start(f32[32,16384]{1,0:T(8,128)} %state_ref.7) | copy-start | bytes 6291460
  1.6 0.7 copy-start.2
  2.3 0.7 copy-start.3
  3.0 0.7 copy-start.4
  3.7 9.3 %copy-start.1 = (f32[32,16384]{1,0:T(8,128)S(1)}, f32[32,16384]{1,0:T(8,128)}, u32[]{:S(2)}) copy-start(f32[32,16384]{1,0:T(8,128)} %state_ref.7) | copy-start | bytes 6291460
  3.7 48.7 %copy-start.9 = (f32[3]{0:T(128)S(1)}, f32[3]{0:T(128)}, u32[]{:S(2)}) copy-start(f32[3]{0:T(128)} %constant.19.clone) | copy-start | bytes 40
  51.5 0.9 copy-start.5
  52.3 17.6 %copy-start.7 = (bf16[32,8192]{1,0:T(8,128)(2,1)}, bf16[32,8192]{1,0:T(8,128)(2,1)S(1)}, u32[]{:S(2)}) copy-start(bf16[32,8192]{1,0:T(8,128)(2,1)S(1)} %get-tuple-element.18.got_ref) | copy-start | bytes 1572868
  53.1 1.1 %copy-start.6 = (bf16[4,768,128]{2,1,0:T(8,128)(2,1)S(1)}, bf16[4,768,128]{2,1,0:T(8,128)(2,1)}, u32[]{:S(2)}) copy-start(bf16[4,768,128]{2,1,0:T(8,128)(2,1)} %copy-done.5) | copy-start | bytes 2359300
  69.9 20.3 %collective-permute-start.1 = (bf16[32,4096]{1,0:T(8,128)(2,1)}, bf16[32,4096]{1,0:T(8,128)(2,1)}, u32[]{:S(2)}, u32[]{:S(2)}) collective-permute-start(bf16[32,4096]{1,0:T(8,128)(2,1)} %get-tuple-element.24), channel_id=1, source_target_pairs={{0,1},{1,0},{2,3},{3,2},{4,5},{5,4},{6,7},{7,6},{8,9},{9,8},{10,11... | collective-permute-start | bytes 786440 | tf_op jit(solution)/shard_map/ppermute | solution.py:446
  71.6 1.0 %copy-start.8 = (bf16[32,8192]{1,0:T(8,128)(2,1)S(1)}, bf16[32,8192]{1,0:T(8,128)(2,1)}, u32[]{:S(2)}) copy-start(bf16[32,8192]{1,0:T(8,128)(2,1)} %copy-done.7) | copy-start | bytes 1572868
  90.2 7.9 %collective-permute-start = (bf16[32,4096]{1,0:T(8,128)(2,1)}, bf16[32,4096]{1,0:T(8,128)(2,1)S(1)}, u32[]{:S(2)}, u32[]{:S(2)}) collective-permute-start(bf16[32,4096]{1,0:T(8,128)(2,1)} %get-tuple-element.23), channel_id=1, source_target_pairs={{0,1},{1,0},{2,3},{3,2},{4,5},{5,4},{6,7},{7,6},{8,9},{9,8},{10,11... | collective-permute-start | bytes 786440 | tf_op jit(solution)/shard_map/ppermute | solution.py:446
where the time goes:
time: 101 us
  Pallas kernels  81 us (80%)
  waiting for transfers between devices  7.85 us (8%)
  local copies, waits for them, and re-layouts  6.81 us (7%)
  other arithmetic  3.37 us (3%)
  starting transfers between devices  1.64 us (2%)
    pallas_call x1, Pallas kernels, shards(): pl.pallas_call(functools.partial(kernel, n_space, batches, obs_dev, half_...  38.5 us
    pallas_call x2, Pallas kernels, shards(): pl.pallas_call(functools.partial(update_kernel, part * part_width), out_s...  33.3 us
    pallas_call x1, Pallas kernels, shards(): pl.pallas_call(gather_kernel, out_shape=(shape((half_members, n_obs), f32...  9.29 us
    ppermute x2, waiting for transfers between devices, shards(): come.append(lax.ppermute(sent, 'mem', [(0, 1), (1, 0)]))  7.85 us
    unnamed x20, local copies, waits for them, and re-layouts  6.72 us
  transfers between devices with their start and end apart: 2, of which 1 were waited for; matrix products, arithmetic and copies ran while one was open for 0% of the time, Pallas kernels for 17%

commit v1 on v0

--- a/solution.py
+++ b/solution.py
@@ -14,11 +14,21 @@
 SPAN = 512
 SIDES = ((1, True), (1, False), (0, False), (2, True))
 GROUP = 64
-PARTS = 2
+PARTS = (3, 1)
 f32, bf16 = jnp.float32, jnp.bfloat16
 
 
-def gather_kernel(idx_ref, state_ref, pos_ref, value_ref, var_ref, out_ref, row_ref):
+def gather_kernel(
+    idx_ref, state_ref, pos_any, value_any, var_any, out_ref, row_ref,
+    pos_ref, value_ref, var_ref, sems,
+):
+    copies = [
+        pltpu.make_async_copy(src, dst, sems.at[i])
+        for i, (src, dst) in enumerate(
+            ((pos_any, pos_ref), (value_any, value_ref), (var_any, var_ref)))
+    ]
+    for copy in copies:
+        copy.start()
     half_members, cols = state_ref.shape
     batches, obs_dev = idx_ref.shape
     base = lax.axis_index("space") * cols
@@ -39,6 +49,9 @@
                     acc = jnp.where(lanes == t, moved, acc)
                 return acc
             parts.append(lax.fori_loop(0, 4, pick, jnp.zeros((half_members, 128), f32)))
+        if batch == 0:
+            for copy in copies:
+                copy.wait()
         q = (pos_ref[batch:batch + 1, :] - base - cols // 2).astype(f32) * (1.0 / RADIUS)
         each = jnp.broadcast_to(q, (obs_dev, obs_dev))
         mine = jnp.transpose(each)
@@ -177,23 +190,31 @@
                 aw[batch, slot, members:2 * members, :], gain, preferred_element_type=f32)
         return total
 
-    def build(batch):
-        def row(o):
-            if o == 0:
-                return pos_own[batch:batch + 1, :]
-            return pos_nb[OFFSETS.index(o), batch:batch + 1, :] + o * block
+    def row(batch, o):
+        if o == 0:
+            return pos_own[batch:batch + 1, :]
+        return pos_nb[OFFSETS.index(o), batch:batch + 1, :] + o * block
+
+    def turn_around(batch, slot):
+        awt_out[batch, slot * obs_dev:(slot + 1) * obs_dev, :] = jnp.transpose(
+            aw[batch, slot].astype(f32)).astype(bf16)
+
+    def build_early(batch):
         for o in (-2, 0, 2):
             slot = SLOT[o]
-            q = row(o)
+            q = row(batch, o)
             c = q if o == 0 else (1.0 + q if o < 0 else 1.0 - q)
             coef[slot] = jnp.transpose(jnp.broadcast_to(c, (CHUNK, obs_dev)))
             c_out[batch, slot:slot + 1, :] = c
-            awt_out[batch, slot * obs_dev:(slot + 1) * obs_dev, :] = jnp.transpose(
-                aw[batch, slot].astype(f32)).astype(bf16)
+        turn_around(batch, SLOT[0])
+
+    def build(batch):
+        turn_around(batch, SLOT[-2])
+        turn_around(batch, SLOT[2])
         sums = 0.0
         for o in (-1, 1):
             slot = SLOT[o]
-            q = row(o)
+            q = row(batch, o)
             c = 1.0 + q if o < 0 else 1.0 - q
             a = aw[batch, slot, :members, :].astype(f32)
             rhs = jnp.concatenate([a * (c * c), a * (2.0 * o * c), a], axis=0).astype(bf16)
@@ -215,6 +236,13 @@
         change = post_mean - obs_mean + (jnp.sqrt(post_var / spread) - 1.0) * anomaly
         aw[batch, SLOT[0], :members, :] = anomaly.astype(bf16)
         aw[batch, SLOT[0], members:, :] = (change / ((members - 1) * spread)).astype(bf16)
+
+    def advance(batch, later):
+        if batch < 0:
+            return
+        span = slice(later * obs_dev, (later + 1) * obs_dev)
+        now = g_ref[:, span]
+        g_ref[:, span] = now + increment(batch, now, pos_own[later:later + 1, :])
 
     for batch in range(batches):
         if batch == 0:
@@ -232,15 +260,16 @@
                 @pl.when(valid[o])
                 def _(o=o):
                     pos_wait(o)
+        for later in range(batch + 1, batches):
+            advance(batch - 1, later)
+        build_early(batch)
         for o in OFFSETS:
             @pl.when(valid[o])
             def _(o=o):
                 aw_wait(batch, o)
         build(batch)
-        for later in range(batch + 1, batches):
-            span = slice(later * obs_dev, (later + 1) * obs_dev)
-            now = g_ref[:, span]
-            g_ref[:, span] = now + increment(batch, now, pos_own[later:later + 1, :])
+        if batch + 1 < batches:
+            advance(batch, batch + 1)
     x_copy.wait_recv()
     got_ref[...] = x_recv[...]
 
@@ -390,8 +419,12 @@
     gathered, rows = pl.pallas_call(
         gather_kernel,
         out_shape=(shape((half_members, n_obs), f32), shape((batches, 8, obs_dev), f32)),
-        in_specs=[smem, vmem, vmem, vmem, vmem],
+        in_specs=[smem, vmem] + [pl.BlockSpec(memory_space=pl.ANY)] * 3,
         out_specs=(vmem, vmem),
+        scratch_shapes=[
+            pltpu.VMEM((batches, obs_dev), jnp.int32), pltpu.VMEM((batches, obs_dev), f32),
+            pltpu.VMEM((batches, obs_dev), f32), dma((3,)),
+        ],
         compiler_params=pltpu.CompilerParams(vmem_limit_bytes=32 * 1024 * 1024),
     )(obs_index, state, obs_index, obs_value, obs_var)
     got, awt, moments, c_rows = pl.pallas_call(
@@ -426,11 +459,12 @@
     low = jnp.sum((turn[:, :, None, :] <= edges).astype(jnp.int32), axis=3)
     high = jnp.sum((turn[:, :, None, :] < edges + (SPAN - 1) / RADIUS).astype(jnp.int32), axis=3)
     bounds = jnp.stack([low, jnp.maximum(low, high)], axis=2).reshape(batches, -1)
-    part_width = width // PARTS
     own, come = [], []
-    for part in range(PARTS):
+    first = 0
+    for part in PARTS:
+        part_width = width * part // sum(PARTS)
         kept, sent = pl.pallas_call(
-            functools.partial(update_kernel, part * part_width),
+            functools.partial(update_kernel, first),
             out_shape=(
                 shape((half_members, part_width), f32), shape((half_members, part_width), bf16)),
             in_specs=[smem] + [vmem] * 5,
@@ -440,8 +474,9 @@
                 pltpu.VMEM((4, obs_dev // GROUP + 1, members, 3 * members), f32)],
             compiler_params=pltpu.CompilerParams(vmem_limit_bytes=32 * 1024 * 1024),
             cost_estimate=pl.CostEstimate(
-                flops=12 * 10**9 // PARTS, bytes_accessed=4 * 2**20, transcendentals=0),
+                flops=12 * 10**9 * part // sum(PARTS), bytes_accessed=4 * 2**20, transcendentals=0),
         )(bounds, state, got, awt, moments, c_rows)
+        first += part_width
         own.append(kept)
         come.append(lax.ppermute(sent, "mem", [(0, 1), (1, 0)]))
     own = jnp.concatenate(own, axis=1)

time: 101 us -> 99.1 us (0.981)
  starting transfers between devices: 1.64 us -> 4.62 us
  Pallas kernels: 81 us -> 78.2 us
  waiting for transfers between devices: 7.85 us -> 5.18 us
    ppermute x2, starting transfers between devices: 1.64 us -> 4.62 us  [shards(): come.append(lax.ppermute(sent, 'mem', [(0, 1), (1, 0)]))]
    ppermute x2, waiting for transfers between devices: 7.85 us -> 5.18 us  [shards(): come.append(lax.ppermute(sent, 'mem', [(0, 1), (1, 0)]))]
    pallas_call x2, Pallas kernels: 33.3 us -> 31.1 us  [shards(): pl.pallas_call(functools.partial(update_kernel, first), out_shape=(shape(...]
    unnamed x20 -> x22, local copies, waits for them, and re-layouts: 6.72 us -> 7.5 us
  transfers between devices with their start and end apart: 2 -> 2, of which waited for: 1 -> 1; matrix products, arithmetic and copies ran while one was open for 0% -> 0% of each run, Pallas kernels for 17% -> 11%
where the time goes in v1:
time: 99.1 us
  Pallas kernels  78.2 us (79%)
  local copies, waits for them, and re-layouts  7.59 us (8%)
  waiting for transfers between devices  5.18 us (5%)
  starting transfers between devices  4.62 us (5%)
  other arithmetic  3.42 us (3%)
    pallas_call x1, Pallas kernels, shards(): pl.pallas_call(functools.partial(kernel, n_space, batches, obs_dev, half_...  37.8 us
    pallas_call x2, Pallas kernels, shards(): pl.pallas_call(functools.partial(update_kernel, first), out_shape=(shape(...  31.1 us
    pallas_call x1, Pallas kernels, shards(): pl.pallas_call(gather_kernel, out_shape=(shape((half_members, n_obs), f32...  9.35 us
    unnamed x22, local copies, waits for them, and re-layouts  7.5 us
    ppermute x2, waiting for transfers between devices, shards(): come.append(lax.ppermute(sent, 'mem', [(0, 1), (1, 0)]))  5.18 us
    ppermute x2, starting transfers between devices, shards(): come.append(lax.ppermute(sent, 'mem', [(0, 1), (1, 0)]))  4.62 us
  transfers between devices with their start and end apart: 2, of which 1 were waited for; matrix products, arithmetic and copies ran while one was open for 0% of the time, Pallas kernels for 11%

profile of v1, /device:TPU:16, one launch (start us, length us, event | category | flops | bytes accessed | tf_op | source)
XLA Modules:
  0.0 99.1 jit_solution(2120022792143715540)
XLA Ops:
  0.0 0.0 copy-start
  0.0 1.6 %copy-done = f32[32,16384]{1,0:T(8,128)S(1)} copy-done((f32[32,16384]{1,0:T(8,128)S(1)}, f32[32,16384]{1,0:T(8,128)}, u32[]{:S(2)}) %copy-start) | copy-done | bytes 2097176
  1.6 0.0 copy-start.2
  1.6 0.7 copy-done.2
  2.3 0.0 copy-start.3
  2.3 0.7 copy-done.3
  3.0 0.0 copy-start.4
  3.0 0.7 copy-done.4
  3.7 0.0 copy-start.1
  3.7 0.0 copy-start.10
  3.7 9.4 %shard_map.55 = (f32[32,1024]{1,0:T(8,128)S(1)}, f32[4,8,256]{2,1,0:T(8,128)S(1)}) custom-call(s32[4,256]{1,0:T(4,128)S(1)} %copy-done.2, f32[32,16384]{1,0:T(8,128)S(1)} %copy-done, s32[4,256]{1,0:T(4,128)S(1)} %copy-done.2, f32[4,256]{1,0:T(4,128)S(1)} %copy-done.3, f32[4,256]{1,0:T(4,128)S(1)} %copy-done.4), custom_call_target="tpu_custom_call" | custom-call | tf_op jit(solution)/shard_map/pallas_call | solution.py:419
  13.0 0.0 copy-done.1
  13.0 37.8 %shard_map.56 = (bf16[32,8192]{1,0:T(8,128)(2,1)S(1)}, bf16[4,768,128]{2,1,0:T(8,128)(2,1)S(1)}, f32[4,64,192]{2,1,0:T(8,128)S(1)}, f32[4,8,256]{2,1,0:T(8,128)S(1)}) custom-call(f32[32,1024]{1,0:T(8,128)S(1)} %get-tuple-element.15.g_send, f32[32,16384]{1,0:T(8,128)S(1)} %copy-done.1, f32[4,8,256]{2,1,0:T(8,128)S(1)} %get-tuple-element.16.row_ref), custom_call_target="tpu_custom_call" | custom-call | tf_op jit(solution)/shard_map/pallas_call | solution.py:430
  50.8 0.0 copy-start.5
  50.8 0.9 copy-done.5
  51.7 0.0 copy-start.7
  51.7 0.8 copy-done.7
  52.5 0.0 copy-done.10
  52.5 0.1 slice_multiply_fusion
  52.6 0.6 convert_reduce_fusion
  53.2 0.1 reshape.27.bound_ref
  53.3 0.0 copy-start.6
  53.3 1.1 %copy-done.6 = bf16[4,768,128]{2,1,0:T(8,128)(2,1)S(1)} copy-done((bf16[4,768,128]{2,1,0:T(8,128)(2,1)S(1)}, bf16[4,768,128]{2,1,0:T(8,128)(2,1)}, u32[]{:S(2)}) %copy-start.6) | copy-done | bytes 786456
  54.4 0.0 copy-start.8
  54.4 1.0 %copy-done.8 = bf16[32,8192]{1,0:T(8,128)(2,1)S(1)} copy-done((bf16[32,8192]{1,0:T(8,128)(2,1)S(1)}, bf16[32,8192]{1,0:T(8,128)(2,1)}, u32[]{:S(2)}) %copy-start.8) | copy-done | bytes 524312
  55.5 0.0 copy-start.9
  55.5 20.4 %shard_map.57 = (f32[32,6144]{1,0:T(8,128)S(1)}, bf16[32,6144]{1,0:T(8,128)(2,1)}) custom-call(s32[4,96]{1,0:T(4,128)S(1)} %reshape.27.bound_ref, f32[32,16384]{1,0:T(8,128)S(1)} %copy-done.1, bf16[32,8192]{1,0:T(8,128)(2,1)S(1)} %copy-done.8, bf16[4,768,128]{2,1,0:T(8,128)(2,1)S(1)} %copy-done.6, f32[4,64,192]{2,1,0:T(8,128)S(1)} %get-tuple-element.20.moment_ref, ...), custom_call_target="tpu_custom_call" | custom-call | flops 8999999488 | bytes 4194304 | tf_op jit(solution)/shard_map/pallas_call | solution.py:466
  75.8 4.6 %collective-permute-start = (bf16[32,6144]{1,0:T(8,128)(2,1)}, bf16[32,6144]{1,0:T(8,128)(2,1)}, u32[]{:S(2)}, u32[]{:S(2)}) collective-permute-start(bf16[32,6144]{1,0:T(8,128)(2,1)} %get-tuple-element.23), channel_id=1, source_target_pairs={{0,1},{1,0},{2,3},{3,2},{4,5},{5,4},{6,7},{7,6},{8,9},{9,8},{10,11... | collective-permute-start | bytes 1179656 | tf_op jit(solution)/shard_map/ppermute | solution.py:481
  80.4 0.0 copy-done.9
  80.4 10.7 %shard_map.58 = (f32[32,2048]{1,0:T(8,128)S(1)}, bf16[32,2048]{1,0:T(8,128)(2,1)}) custom-call(s32[4,96]{1,0:T(4,128)S(1)} %reshape.27.bound_ref, f32[32,16384]{1,0:T(8,128)S(1)} %copy-done.1, bf16[32,8192]{1,0:T(8,128)(2,1)S(1)} %copy-done.9, bf16[4,768,128]{2,1,0:T(8,128)(2,1)S(1)} %copy-done.6, f32[4,64,192]{2,1,0:T(8,128)S(1)} %get-tuple-element.20.moment_ref, ...), custom_call_target="tpu_custom_call" | custom-call | flops 3000000000 | bytes 4194304 | tf_op jit(solution)/shard_map/pallas_call | solution.py:466
  91.1 0.0 collective-permute-start.1
  91.1 5.2 %collective-permute-done.1 = bf16[32,2048]{1,0:T(8,128)(2,1)S(1)} collective-permute-done((bf16[32,2048]{1,0:T(8,128)(2,1)}, bf16[32,2048]{1,0:T(8,128)(2,1)S(1)}, u32[]{:S(2)}, u32[]{:S(2)}) %collective-permute-start.1) | collective-permute-done | bytes 131104 | tf_op jit(solution)/shard_map/ppermute | solution.py:481
  96.3 0.0 collective-permute-done
  96.3 1.2 %convert_add_fusion = (f32[32,8192]{1,0:T(8,128)S(1)}, f32[32,8192]{1,0:T(8,128)S(1)}) fusion(f32[32,16384]{1,0:T(8,128)S(1)} %copy-done.1, bf16[32,2048]{1,0:T(8,128)(2,1)S(1)} %collective-permute-done.1, bf16[32,6144]{1,0:T(8,128)(2,1)} %collective-permute-done), kind=kLoop, calls=%fused_computation.1 | loop fusion | flops 1572864 | bytes 4718592 | tf_op jit(solution)/shard_map/add | solution.py:487
  97.5 1.6 %maximum_select_fusion = f32[32,16384]{1,0:T(8,128)} fusion(f32[32,8192]{1,0:T(8,128)S(1)} %get-tuple-element.30, f32[32,2048]{1,0:T(8,128)S(1)} %get-tuple-element.22, f32[32,6144]{1,0:T(8,128)S(1)} %get-tuple-element.21, f32[32,8192]{1,0:T(8,128)S(1)} %get-tuple-element.29, pred[]{:T(512)S(6)} %eq.3), kind=kLoop, calls=%fused_computation | loop fusion | flops 2621440 | bytes 5242881 | tf_op jit(solution)/shard_map/jit(_where)/select_n | solution.py:484
  (4 shorter events, 0.0 us)
Async XLA Ops:
  0.0 1.6 %copy-start = (f32[32,16384]{1,0:T(8,128)S(1)}, f32[32,16384]{1,0:T(8,128)}, u32[]{:S(2)}) copy-start(f32[32,16384]{1,0:T(8,128)} %state_ref.7) | copy-start | bytes 6291460
  1.6 0.7 copy-start.2
  2.3 0.7 copy-start.3
  3.0 0.7 copy-start.4
  3.7 9.4 %copy-start.1 = (f32[32,16384]{1,0:T(8,128)S(1)}, f32[32,16384]{1,0:T(8,128)}, u32[]{:S(2)}) copy-start(f32[32,16384]{1,0:T(8,128)} %state_ref.7) | copy-start | bytes 6291460
  3.7 48.8 %copy-start.10 = (f32[3]{0:T(128)S(1)}, f32[3]{0:T(128)}, u32[]{:S(2)}) copy-start(f32[3]{0:T(128)} %constant.19.clone) | copy-start | bytes 40
  50.8 0.9 copy-start.5
  51.7 0.8 copy-start.7
  53.3 1.1 %copy-start.6 = (bf16[4,768,128]{2,1,0:T(8,128)(2,1)S(1)}, bf16[4,768,128]{2,1,0:T(8,128)(2,1)}, u32[]{:S(2)}) copy-start(bf16[4,768,128]{2,1,0:T(8,128)(2,1)} %copy-done.5) | copy-start | bytes 2359300
  54.4 1.0 %copy-start.8 = (bf16[32,8192]{1,0:T(8,128)(2,1)S(1)}, bf16[32,8192]{1,0:T(8,128)(2,1)}, u32[]{:S(2)}) copy-start(bf16[32,8192]{1,0:T(8,128)(2,1)} %copy-done.7) | copy-start | bytes 1572868
  55.5 25.0 %copy-start.9 = (bf16[32,8192]{1,0:T(8,128)(2,1)S(1)}, bf16[32,8192]{1,0:T(8,128)(2,1)}, u32[]{:S(2)}) copy-start(bf16[32,8192]{1,0:T(8,128)(2,1)} %copy-done.7) | copy-start | bytes 1572868
  75.8 20.5 %collective-permute-start = (bf16[32,6144]{1,0:T(8,128)(2,1)}, bf16[32,6144]{1,0:T(8,128)(2,1)}, u32[]{:S(2)}, u32[]{:S(2)}) collective-permute-start(bf16[32,6144]{1,0:T(8,128)(2,1)} %get-tuple-element.23), channel_id=1, source_target_pairs={{0,1},{1,0},{2,3},{3,2},{4,5},{5,4},{6,7},{7,6},{8,9},{9,8},{10,11... | collective-permute-start | bytes 1179656 | tf_op jit(solution)/shard_map/ppermute | solution.py:481
  91.1 5.2 %collective-permute-start.1 = (bf16[32,2048]{1,0:T(8,128)(2,1)}, bf16[32,2048]{1,0:T(8,128)(2,1)S(1)}, u32[]{:S(2)}, u32[]{:S(2)}) collective-permute-start(bf16[32,2048]{1,0:T(8,128)(2,1)} %get-tuple-element.24), channel_id=1, source_target_pairs={{0,1},{1,0},{2,3},{3,2},{4,5},{5,4},{6,7},{7,6},{8,9},{9,8},{10,11... | collective-permute-start | bytes 393224 | tf_op jit(solution)/shard_map/ppermute | solution.py:481
